TPU v7x, 32 devices: a whole 2x2x4 slice. The times are simulated.
32 devices in a mesh: dp: 16 (over z, y, x), tensor: 2 (over core).
Axes of the slice: x: 2, y: 2, z: 4, core: 2. Of those that a mesh axis runs over, the one named last changes fastest.
Arguments:
- inputs: bfloat16 [8192, 768], P(('dp', 'tensor')), may hold values from -6 to 6
- segments: int32 [8192], P('dp'), may hold values from 0 to 2, as said below
- gain_first: float32 [768], P(('dp', 'tensor')), may hold values from 0.5 to 1.5
- gain_second: float32 [768], P(('dp', 'tensor')), may hold values from 0.5 to 1.5
- attend_weight: bfloat16 [3, 768, 768], P(None, 'dp', 'tensor'), may hold values from -0.21875 to 0.21875
- mixing_matrix: bfloat16 [768, 768], P('dp', 'tensor'), may hold values from -0.875 to 0.875
- expand_matrix: bfloat16 [2, 768, 1152], P(None, 'dp', 'tensor'), may hold values from -0.21875 to 0.21875
- reduce_matrix: bfloat16 [768, 1152], P('dp', 'tensor'), may hold values from -0.1875 to 0.1875
- cotangent: bfloat16 [8192, 768], P(('dp', 'tensor')), may hold values from -6 to 6
Outputs:
- output: bfloat16 [8192, 768], P(('dp', 'tensor'))
- input_grad: float32 [8192, 768], P(('dp', 'tensor'))
- first_grad: float32 [768], P(('dp', 'tensor'))
- second_grad: float32 [768], P(('dp', 'tensor'))
- attend_grad: float32 [3, 768, 768], P(None, 'dp', 'tensor')
- mixing_grad: float32 [768, 768], P('dp', 'tensor')
- expand_grad: float32 [2, 768, 1152], P(None, 'dp', 'tensor')
- reduce_grad: float32 [768, 1152], P('dp', 'tensor')
Inputs may be any that keep to these rules, and one draw needn't show every extreme that they name: `segments`: in each aligned block of 512 tokens (one sequence) the numbers start at 0, never fall and rise by one at two places, so each sequence holds three documents of 128 tokens or more; the middle one covers positions 255 and 256 of its sequence.
All inputs are finite; a program needn't handle non-finite values.
Results may differ from a plain program's by a relative error of at most 0.018.
Values may be sent and summed in bfloat16 or wider, within the bound.
A program may use at most 128 MiB of HBM per device.

v0:
```python
import functools
import math

import jax
import jax.numpy as jnp
import numpy as np
from jax import lax
from jax.experimental import pallas as pl
from jax.experimental.pallas import tpu as pltpu
from jax.sharding import PartitionSpec as P

HEAD_SIZE = 64
EPS = 1e-05
THETA = 160000.0
MASKED = -1e30
LANES = 128
VMEM_LIMIT = 60 * 1024 * 1024
MESH = pl.DeviceIdType.MESH
VMEM = pltpu.VMEM


def normalize(values):
    centered = values - jnp.mean(values, axis=-1, keepdims=True)
    inverse_std = lax.rsqrt(jnp.mean(centered * centered, axis=-1, keepdims=True) + EPS)
    return (centered * inverse_std, inverse_std)


def normalize_back(grad_unit, unit_rows, inverse_std):
    plain_mean = jnp.mean(grad_unit, axis=-1, keepdims=True)
    cross_mean = jnp.mean(grad_unit * unit_rows, axis=-1, keepdims=True)
    return inverse_std * (grad_unit - plain_mean - unit_rows * cross_mean)


def plain(left_side, right_side):
    return jnp.dot(left_side, right_side, preferred_element_type=jnp.float32)


def contract_last(left_side, right_side):
    return lax.dot_general(
        left_side, right_side, (((1,), (1,)), ((), ())), preferred_element_type=jnp.float32
    )


def contract_first(left_side, right_side):
    return lax.dot_general(
        left_side, right_side, (((0,), (0,)), ((), ())), preferred_element_type=jnp.float32
    )


def gelu_slope(values):
    return 0.5 * (1.0 + lax.erf(values / math.sqrt(2.0))) + values * jnp.exp(
        -0.5 * values * values
    ) / math.sqrt(2.0 * math.pi)


def position():
    dp, core = lax.axis_index("dp"), lax.axis_index("tensor")
    zh, zl = lax.rem(lax.div(dp, 8), 2), lax.rem(lax.div(dp, 4), 2)
    y, x = lax.rem(lax.div(dp, 2), 2), lax.rem(dp, 2)
    peers = dict(
        core=(dp, 1 - core),
        x=(dp + 1 - 2 * x, core),
        y=(dp + 2 - 4 * y, core),
        zl=(dp + 4 - 8 * zl, core),
        zh=(dp + 8 - 16 * zh, core),
    )
    return core, zh, zl, y, x, peers


def greet(peers):
    barrier = pltpu.get_barrier_semaphore()
    for peer in peers.values():
        pl.semaphore_signal(barrier, inc=1, device_id=peer, device_id_type=MESH)
    pl.semaphore_wait(barrier, len(peers))


class Chunk:
    def __init__(self, groups, landed=None, first=None):
        self.groups, self.landed, self.first, self.stage = groups, landed, first, 0

    def advance(self):
        stage = self.stage
        if stage > len(self.groups):
            return
        if stage > 0:
            for copy in self.groups[stage - 1]:
                copy.wait_recv()
            if self.landed is not None:
                self.landed(stage - 1)
        if stage == 1 and self.first is not None:
            self.first.wait()
        if stage < len(self.groups):
            for copy in self.groups[stage]:
                copy.start()
        self.stage = stage + 1

    def finish(self):
        while self.stage <= len(self.groups):
            self.advance()

    def wait_sent(self):
        for group in self.groups:
            for copy in group:
                copy.wait_send()


def remote_maker(send_sem, recv_sem, peers):
    def remote(k, slot, source, target, peer):
        return pltpu.make_async_remote_copy(
            src_ref=source,
            dst_ref=target,
            send_sem=send_sem.at[k, slot],
            recv_sem=recv_sem.at[k, slot],
            device_id=peers[peer],
            device_id_type=MESH,
        )

    return remote


def vector_chunk(remote, k, start, totals, arrived):
    order = ("zh", "zl", "y", "x", "core")
    sources = [start] + [totals.at[i] for i in range(4)]
    groups = [
        [remote(k, i, sources[i], arrived.at[i], peer)] for i, peer in enumerate(order)
    ]

    def landed(i):
        totals[i] = (start[...] if i == 0 else totals[i - 1]) + arrived[i]

    return Chunk(groups, landed)


LAG = 2


def gather_groups(remote, k, shard, full, j, route, at):
    core, zh, zl, y, x = at
    every = slice(None)

    def same(slot, index, peer):
        block = full.at[(core, j) + index]
        return remote(k, slot, block, block, peer)

    start = [remote(k, 0, shard.at[j], full.at[core, j, zh, zl, y, x], "zh")]
    if route == "plane":
        middle = [
            [same(1, (every, zl, y, x), "zl")],
            [same(2, (every, 0, y, x), "x"), same(3, (every, 1, y, x), "y")],
            [same(4, (every, 0, y), "y"), same(5, (every, 1, every, x), "x")],
        ]
    elif route == "x":
        middle = [
            [same(1, (every, zl, y, x), "x")],
            [same(2, (every, zl, y), "y")],
            [same(3, (every, zl), "zl")],
        ]
    else:
        middle = [
            [same(1, (every, zl, y, x), "y")],
            [same(2, (every, zl, every, x), "x")],
            [same(3, (every, zl), "zl")],
        ]
    return [start] + middle + [[same(6, (), "core")]]


def reduce_chunk(remote, k, j, route, at, part, store, total, one, two, three, four):
    core, zh, zl, y, x = at
    every = slice(None)
    here = total.at[j]
    start = [remote(k, 0, part.at[1 - core, j], here, "core")]
    last = [remote(k, 6, here.at[1 - zh, zl, y, x], four.at[j], "zh")]
    if route == "plane":
        middle = [
            [
                remote(k, 1, here.at[every, 0, every, 1 - x], one.at[j, 0], "x"),
                remote(k, 2, here.at[every, 1, 1 - y], one.at[j, 1], "y"),
            ],
            [
                remote(k, 3, here.at[every, 0, 1 - y, x], two.at[j, 0], "y"),
                remote(k, 4, here.at[every, 1, y, 1 - x], two.at[j, 1], "x"),
            ],
            [remote(k, 5, here.at[every, 1 - zl, y, x], three.at[j], "zl")],
        ]
    elif route == "x":
        middle = [
            [remote(k, 1, here.at[every, 1 - zl], one.at[j], "zl")],
            [remote(k, 3, here.at[every, zl, 1 - y], two.at[j], "y")],
            [remote(k, 5, here.at[every, zl, y, 1 - x], three.at[j], "x")],
        ]
    else:
        middle = [
            [remote(k, 1, here.at[every, 1 - zl], one.at[j], "zl")],
            [remote(k, 3, here.at[every, zl, every, 1 - x], two.at[j], "x")],
            [remote(k, 5, here.at[every, zl, 1 - y, x], three.at[j], "y")],
        ]

    def bits(b):
        return lax.div(b, 4), lax.rem(lax.div(b, 2), 2), lax.rem(b, 2)

    def plus(index, value):
        total[(j,) + index] = total[(j,) + index] + value

    def landed(stage):
        if stage == 0:

            @pl.loop(0, 16)
            def _(b):
                index = (lax.div(b, 8),) + bits(lax.rem(b, 8))
                plus(index, part[(core, j) + index])

        elif stage == 1:

            @pl.loop(0, 8)
            def _(b):
                p, q, r = bits(b)
                if route == "plane":
                    @pl.when(p == 0)
                    def _():
                        plus((q, 0, r, x), one[j, 0, q, r])

                    @pl.when(p == 1)
                    def _():
                        plus((q, 1, y, r), one[j, 1, q, r])

                else:
                    plus((p, zl, q, r), one[j, p, q, r])

        elif stage == 2:

            @pl.loop(0, 4)
            def _(b):
                _, p, q = bits(b)
                if route == "plane":
                    plus((q, p, y, x), two[j, p, q])
                elif route == "x":
                    plus((p, zl, y, q), two[j, p, q])
                else:
                    plus((p, zl, q, x), two[j, p, q])

        elif stage == 3:

            @pl.loop(0, 2)
            def _(hi):
                plus((hi, zl, y, x), three[j, hi])

        else:
            store(total[j, zh, zl, y, x].astype(jnp.float32) + four[j].astype(jnp.float32))

    return Chunk([start] + middle + [last], landed)


def layer_kernel(
    gain_part, attend_w, mixing_w, expand_w, reduce_w, tokens, cotangent, cosine, sine, seg_rows,
    seg_cols,
    output, input_out, gain_out, attend_out, mixing_out, expand_out, reduce_out,
    attend_full, mixing_full, expand_full, reduce_full, attend_part, expand_part, reduce_part,
    sum_a, sum_e, sum_r, one_a, one_e, one_r, two_a, two_e, two_r, three_a, three_e, three_r,
    four_a, four_e, four_r,
    other_tokens, rows, other_rows, totals, arrived, vector, grad_totals, grad_arrived,
    cos, sin, normed, unit, inverse, queries, keys, values, mixed, logs, middle, unit_two,
    normed_two, normed_two_grad, grad_middle, branch, normed_grad,
    own_sem, send_sem, recv_sem, back_send_sem, back_recv_sem, pair_sem,
):
    core, zh, zl, y, x, peers = position()
    at = (core, zh, zl, y, x)
    own, width = tokens.shape
    pairs = width // LANES
    side_pairs = pairs // 2
    remote = remote_maker(send_sem, recv_sem, peers)
    back = remote_maker(back_send_sem, back_recv_sem, peers)

    pieces = [
        (attend_w, attend_full, 0, "plane"), (attend_w, attend_full, 1, "plane"),
        (attend_w, attend_full, 2, "x"), (mixing_w, mixing_full, 0, "plane"),
        (expand_w, expand_full, 0, "x"), (expand_w, expand_full, 1, "y"),
        (reduce_w, reduce_full, 0, "plane"),
    ]
    chunks = [vector_chunk(remote, 0, gain_part, totals, arrived)]
    for k, (shard, full, j, route) in enumerate(pieces, 1):
        local = pltpu.make_async_copy(
            shard.at[j], full.at[core, j, zh, zl, y, x], own_sem.at[k]
        )
        local.start()
        chunks.append(Chunk(gather_groups(remote, k, shard, full, j, route, at), first=local))

    def pair_copy(i, source, target):
        return pltpu.make_async_remote_copy(
            src_ref=source,
            dst_ref=target,
            send_sem=pair_sem.at[2 * i],
            recv_sem=pair_sem.at[2 * i + 1],
            device_id=peers["core"],
            device_id_type=MESH,
        )

    token_copy = pair_copy(0, tokens, other_tokens)
    row_copy = pair_copy(1, rows, other_rows)
    greet(peers)
    token_copy.start()

    def own_unit():
        mine, others = pl.ds(core * own, own), pl.ds((1 - core) * own, own)
        cos[:own], sin[:own] = cosine[mine], sine[mine]
        cos[own:], sin[own:] = cosine[others], sine[others]
        unit[:own], inverse[:own] = normalize(tokens[...].astype(jnp.float32))

    def other_unit():
        token_copy.wait_recv()
        unit[own:], inverse[own:] = normalize(other_tokens[...].astype(jnp.float32))

    def norm():
        normed[...] = (unit[...] * totals[4, 0:1]).astype(jnp.bfloat16)

    def attend_weights(side, g):
        lanes = slice(g * LANES, (g + 1) * LANES)
        return (attend_full[side, j, :, :, :, :, :, lanes].reshape(-1, LANES) for j in range(3))

    def heads(p):
        def run():
            wq, wk, wv = attend_weights(p // side_pairs, p % side_pairs)
            queries[p], keys[p], values[p], mixed[p], logs[p] = attend_step(
                normed[:own], normed[...], wq, wk, wv, cos[...], sin[...],
                seg_rows[...] == seg_cols[...],
            )

        return run

    def mix():
        summed = tokens[...].astype(jnp.float32)
        for side in range(2):
            columns = [mixed[side * side_pairs + g] for g in range(side_pairs)]
            weight = mixing_full[side, 0].reshape(width, -1)
            summed = summed + contract_last(jnp.concatenate(columns, axis=1), weight)
        middle[...] = summed

    events = [(k + LAG * s, chunk.advance) for k, chunk in enumerate(chunks) for s in range(6)]
    events += [(4.5, own_unit), (7.5, other_unit), (5 * LAG + 0.5, norm)]
    begin = 3 + 5 * LAG
    events += [(begin + 0.1 + 0.65 * p, heads(p)) for p in range(pairs)] + [(begin + 3.6, mix)]
    for _, event in sorted(events, key=lambda e: e[0]):
        event()

    unit_rows, inverse_two = normalize(middle[...])
    unit_two[...] = unit_rows
    normed_two[...] = (unit_rows * totals[4, 1:2]).astype(jnp.bfloat16)

    def feed(side, initial):
        weight_a, weight_g = (expand_full[side, j].reshape(width, -1) for j in range(2))
        weight_r = reduce_full[side, 0].reshape(width, -1)
        activated_in = plain(normed_two[...], weight_a)
        gate_linear = plain(normed_two[...], weight_g)
        spread = 0.5 * (1.0 + lax.erf(activated_in * math.sqrt(0.5)))
        gelu_value = activated_in * spread
        slope = spread + activated_in * jnp.exp(-0.5 * activated_in * activated_in) * (
            1.0 / math.sqrt(2.0 * math.pi)
        )
        hidden = (gelu_value * gate_linear).astype(jnp.bfloat16)
        grad_hidden = plain(cotangent[...], weight_r)
        grad_activated = (grad_hidden * gate_linear * slope).astype(jnp.bfloat16)
        grad_gate = (grad_hidden * gelu_value).astype(jnp.bfloat16)

        def split(value):
            return value.astype(jnp.bfloat16).reshape((2, 2, 2, 2, -1) + value.shape[1:])

        reduce_part[side, 0] = split(contract_first(cotangent[...], hidden))
        expand_part[side, 0] = split(contract_first(normed_two[...], grad_activated))
        expand_part[side, 1] = split(contract_first(normed_two[...], grad_gate))
        middle[...] += contract_last(hidden, weight_r)
        back_rows = contract_last(grad_activated, weight_a) + contract_last(grad_gate, weight_g)
        if initial:
            normed_two_grad[...] = back_rows
        else:
            normed_two_grad[...] += back_rows

    def store_plain(out, j):
        def store(value):
            out[j] = value

        return store

    def store_heads(g):
        lanes, share = slice(g * LANES, (g + 1) * LANES), mixing_out.shape[1]

        def store(value):
            for j in range(3):
                attend_out[j, :, lanes] = value[j * share : (j + 1) * share]
            mixing_out[0, :, lanes] = value[3 * share :]

        return store

    reduce_back = reduce_chunk(
        back, 0, 0, "plane", at, reduce_part, store_plain(reduce_out, 0), sum_r, one_r, two_r,
        three_r, four_r,
    )
    expand_back = [
        reduce_chunk(
            back, 1 + j, j, "xy"[j], at, expand_part, store_plain(expand_out, j), sum_e, one_e,
            two_e, three_e, four_e,
        )
        for j in range(2)
    ]
    attend_back_chunks = [
        reduce_chunk(
            back, 3 + g, g, ("plane", "x", "plane")[g], at, attend_part, store_heads(g), sum_a,
            one_a, two_a, three_a, four_a,
        )
        for g in range(side_pairs)
    ]
    gain_back = vector_chunk(back, 6, vector, grad_totals, grad_arrived)
    feed_chunks = [reduce_back] + expand_back

    def advance(*some):
        for chunk in some:
            chunk.advance()

    feed(1 - core, True)
    advance(*feed_chunks)
    feed(core, False)
    advance(*feed_chunks)
    output[...] = middle[...].astype(output.dtype)
    grad_rows = normed_two_grad[...]
    second_local = jnp.sum(grad_rows * unit_two[...], axis=0, keepdims=True)
    grad_middle[...] = cotangent[...].astype(jnp.float32) + normalize_back(
        grad_rows * totals[4, 1:2], unit_two[...], inverse_two
    )
    branch[...] = grad_middle[...].astype(jnp.bfloat16)

    def heads_back(side, g, initial):
        p = side * side_pairs + g
        wq, wk, wv = attend_weights(side, g)
        lanes = slice(g * LANES, (g + 1) * LANES)
        weights, update, first = attend_back_step(
            normed[:own], normed[...], branch[...], wq, wk, wv,
            mixing_full[side, 0, :, :, :, :, :, lanes].reshape(-1, LANES),
            cos[...], sin[...], seg_rows[...] == seg_cols[...],
            queries[p], keys[p], values[p], mixed[p], logs[p],
        )
        share = mixing_out.shape[1]
        for j, block in enumerate(weights):
            spot = slice(j * share, (j + 1) * share)
            attend_part[side, g, :, :, :, :, spot, :] = block.reshape(2, 2, 2, 2, share, LANES)
        if initial:
            normed_grad[...] = update
        else:
            normed_grad[...] += update
        normed_grad[:own] += first

    a0, a1, a2 = attend_back_chunks
    heads_back(1 - core, 0, True)
    advance(a0, *feed_chunks)
    heads_back(core, 0, False)
    advance(*feed_chunks)
    heads_back(1 - core, 1, False)
    advance(a1, *feed_chunks, a0)
    heads_back(core, 1, False)
    advance(*feed_chunks, a0, a1)
    heads_back(1 - core, 2, False)
    advance(a2, a0, a1, *feed_chunks)
    heads_back(core, 2, False)
    advance(a2, a1, a0)
    vector[...] = jnp.zeros_like(vector)
    vector[0:1] = jnp.sum(normed_grad[...] * unit[...], axis=0, keepdims=True)
    vector[1:2] = second_local
    advance(gain_back)
    gain = totals[4, 0:1]
    rows[...] = normalize_back(normed_grad[own:] * gain, unit[own:], inverse[own:]).astype(
        jnp.bfloat16
    )
    row_copy.start()
    advance(a0, a1, a2, gain_back)
    input_out[...] = grad_middle[...] + normalize_back(
        normed_grad[:own] * gain, unit[:own], inverse[:own]
    )
    backs = [a0, a1, a2, gain_back] + feed_chunks
    for _ in range(6):
        advance(*backs)
    gain_out[...] = grad_totals[4]
    row_copy.wait_recv()
    input_out[...] += other_rows[...].astype(jnp.float32)
    for chunk in chunks + backs:
        chunk.wait_sent()
    token_copy.wait_send()
    row_copy.wait_send()


def layer(gain_part, shards, tokens, cotangent, cosine, sine, seg_rows, seg_cols):
    own, width = tokens.shape
    length, pairs = 2 * own, width // LANES
    full, low = jnp.float32, jnp.bfloat16
    fulls = [VMEM((2, s.shape[0], 2, 2, 2, 2) + s.shape[1:], low) for s in shards]
    share, hidden = shards[2].shape[1:]
    parts = [
        (pairs // 2, 4 * share, LANES), (2, share, hidden), (1, share, hidden),
    ]

    def buffers(dims):
        return [VMEM(p[:1] + dims + p[1:], low) for p in parts]

    def rows(count, columns, dtype):
        return VMEM((count, columns), dtype)

    def stack(count, dtype):
        return VMEM((pairs, count, LANES), dtype)

    vectors = VMEM((5,) + gain_part.shape, full)
    whole = pl.BlockSpec(memory_space=VMEM)
    anywhere = pl.BlockSpec(memory_space=pl.ANY)
    dma = pltpu.SemaphoreType.DMA
    return pl.pallas_call(
        layer_kernel,
        out_shape=[
            jax.ShapeDtypeStruct((own, width), low),
            jax.ShapeDtypeStruct((own, width), full),
            jax.ShapeDtypeStruct(gain_part.shape, full),
        ]
        + [jax.ShapeDtypeStruct(s.shape, full) for s in shards],
        in_specs=[whole] + [anywhere] * 4 + [whole] * 6,
        out_specs=[whole] * 7,
        scratch_shapes=fulls
        + [VMEM((2,) + p[:1] + (2, 2, 2, 2) + p[1:], low) for p in parts]
        + buffers((2, 2, 2, 2))
        + buffers((2, 2, 2))
        + buffers((2, 2))
        + buffers((2,))
        + buffers(())
        + [rows(own, width, low)] * 3
        + [vectors, vectors, VMEM(gain_part.shape, full), vectors, vectors]
        + [rows(length, LANES, full)] * 2
        + [rows(length, width, low), rows(length, width, full), rows(length, 1, full)]
        + [stack(own, low), stack(length, low), stack(length, low), stack(own, low)]
        + [stack(own, full), rows(own, width, full), rows(own, width, full)]
        + [rows(own, width, low), rows(own, width, full), rows(own, width, full)]
        + [rows(own, width, low), rows(length, width, full)]
        + [dma((8,)), dma((8, 7)), dma((8, 7)), dma((7, 7)), dma((7, 7)), dma((4,))],
        compiler_params=pltpu.CompilerParams(
            collective_id=0, has_side_effects=True, vmem_limit_bytes=VMEM_LIMIT
        ),
    )(gain_part, *shards, tokens, cotangent, cosine, sine, seg_rows, seg_cols)


def half_turn(values):
    lane = lax.broadcasted_iota(jnp.int32, values.shape, 1)
    low = lax.rem(lane, HEAD_SIZE) < HEAD_SIZE // 2
    shift = HEAD_SIZE // 2
    return jnp.where(
        low, -pltpu.roll(values, LANES - shift, 1), pltpu.roll(values, shift, 1)
    )


def attend_step(normed_own, normed, wq, wk, wv, cos, sin, allowed):
    own = normed_own.shape[0]
    query = plain(normed_own, wq)
    query = query * cos[:own] + half_turn(query) * sin[:own]
    query = (query * HEAD_SIZE**-0.5).astype(jnp.bfloat16)
    keys = plain(normed, wk)
    keys = (keys * cos + half_turn(keys) * sin).astype(jnp.bfloat16)
    value = plain(normed, wv).astype(jnp.bfloat16)
    mixed, logs = [], []
    for head in range(LANES // HEAD_SIZE):
        part = slice(head * HEAD_SIZE, (head + 1) * HEAD_SIZE)
        scores = jnp.where(allowed, contract_last(query[:, part], keys[:, part]), MASKED)
        peak = jnp.max(scores, axis=-1, keepdims=True)
        exponent = jnp.exp(scores - peak)
        total = jnp.sum(exponent, axis=-1, keepdims=True)
        probs = (exponent / total).astype(jnp.bfloat16)
        mixed.append(plain(probs, value[:, part]).astype(jnp.bfloat16))
        logs.append(jnp.broadcast_to(peak + jnp.log(total), (own, HEAD_SIZE)))
    return query, keys, value, jnp.concatenate(mixed, axis=1), jnp.concatenate(logs, axis=1)


def attend_back_step(
    normed_own, normed, branch, wq, wk, wv, mix, cos, sin, allowed, query, keys, value, attended,
    logs,
):
    own = normed_own.shape[0]
    grad = plain(branch, mix).astype(jnp.bfloat16)
    grad_q, grad_k, grad_v = [], [], []
    for head in range(LANES // HEAD_SIZE):
        part = slice(head * HEAD_SIZE, (head + 1) * HEAD_SIZE)
        qh, kh, vh, gh = query[:, part], keys[:, part], value[:, part], grad[:, part]
        scores = jnp.where(allowed, contract_last(qh, kh), MASKED)
        probs = jnp.exp(scores - logs[:, head * HEAD_SIZE : head * HEAD_SIZE + 1])
        grad_v.append(contract_first(probs.astype(jnp.bfloat16), gh))
        grad_probs = contract_last(gh, vh)
        inner = jnp.sum(grad_probs * probs, axis=-1, keepdims=True)
        grad_scores = (probs * (grad_probs - inner)).astype(jnp.bfloat16)
        grad_q.append(plain(grad_scores, kh))
        grad_k.append(contract_first(grad_scores, qh))
    gq = jnp.concatenate(grad_q, axis=1) * HEAD_SIZE**-0.5
    gk = jnp.concatenate(grad_k, axis=1)
    gv = jnp.concatenate(grad_v, axis=1).astype(jnp.bfloat16)
    gq = (gq * cos[:own] - half_turn(gq * sin[:own])).astype(jnp.bfloat16)
    gk = (gk * cos - half_turn(gk * sin)).astype(jnp.bfloat16)
    weights = (
        contract_first(normed_own, gq).astype(jnp.bfloat16),
        contract_first(normed, gk).astype(jnp.bfloat16),
        contract_first(normed, gv).astype(jnp.bfloat16),
        contract_first(branch, attended).astype(jnp.bfloat16),
    )
    update = contract_last(gk, wk) + contract_last(gv, wv)
    return weights, update, contract_last(gq, wq)


def attend_kernel(
    normed, wq, wk, wv, cosine, sine, seg_rows, seg_cols, q_out, k_out, v_out, att_out, log_out
):
    own = seg_rows.shape[0]
    q_out[0], k_out[0], v_out[0], att_out[0], log_out[0] = attend_step(
        normed[:own], normed[...], wq[0, 0], wk[0, 0], wv[0, 0], cosine[...], sine[...],
        seg_rows[...] == seg_cols[...],
    )


def attend_back_kernel(
    normed, branch, wq, wk, wv, mix, cosine, sine, seg_rows, seg_cols, q_in, k_in, v_in, att_in,
    log_in, weight_out, mix_out, normed_out,
):
    own = seg_rows.shape[0]
    step = pl.program_id(0)
    weights, update, first = attend_back_step(
        normed[:own], normed[...], branch[...], wq[0, 0], wk[0, 0], wv[0, 0], mix[0, 0],
        cosine[...], sine[...], seg_rows[...] == seg_cols[...], q_in[0], k_in[0], v_in[0],
        att_in[0], log_in[0],
    )
    for j in range(3):
        weight_out[0, j] = weights[j]
    mix_out[0, 0] = weights[3]

    @pl.when(step == 0)
    def _():
        normed_out[...] = update

    @pl.when(step > 0)
    def _():
        normed_out[...] += update

    normed_out[:own] += first


def attention_specs(width, own, length, groups):
    def weight(j):
        return pl.BlockSpec((1, 1, width, LANES), lambda p: (p // groups, j, 0, p % groups))

    def columns(rows):
        return pl.BlockSpec((1, rows, LANES), lambda p: (p, 0, 0))

    def whole(*shape):
        return pl.BlockSpec(shape, lambda p: (0,) * len(shape))

    return weight, columns, whole


def attend(normed, weights, cosine, sine, seg_rows, seg_cols):
    length, width = normed.shape
    own = seg_rows.shape[0]
    groups = weights.shape[3] // LANES
    weight, columns, whole = attention_specs(width, own, length, groups)
    pairs = 2 * groups
    return pl.pallas_call(
        attend_kernel,
        grid=(2 * groups,),
        out_shape=[
            jax.ShapeDtypeStruct((pairs, own, LANES), jnp.bfloat16),
            jax.ShapeDtypeStruct((pairs, length, LANES), jnp.bfloat16),
            jax.ShapeDtypeStruct((pairs, length, LANES), jnp.bfloat16),
            jax.ShapeDtypeStruct((pairs, own, LANES), jnp.bfloat16),
            jax.ShapeDtypeStruct((pairs, own, LANES), jnp.float32),
        ],
        in_specs=[
            whole(length, width), weight(0), weight(1), weight(2), whole(length, LANES),
            whole(length, LANES), whole(own, 1), whole(1, length),
        ],
        out_specs=[columns(own), columns(length), columns(length), columns(own), columns(own)],
        compiler_params=pltpu.CompilerParams(vmem_limit_bytes=VMEM_LIMIT),
    )(normed, weights, weights, weights, cosine, sine, seg_rows, seg_cols)


def attend_back(normed, branch, weights, mixing, cosine, sine, seg_rows, seg_cols, saved):
    length, width = normed.shape
    own = seg_rows.shape[0]
    groups = weights.shape[3] // LANES
    weight, columns, whole = attention_specs(width, own, length, groups)
    return pl.pallas_call(
        attend_back_kernel,
        grid=(2 * groups,),
        out_shape=[
            jax.ShapeDtypeStruct((2, 3, width, groups * LANES), jnp.bfloat16),
            jax.ShapeDtypeStruct((2, 1, width, groups * LANES), jnp.bfloat16),
            jax.ShapeDtypeStruct((length, width), jnp.float32),
        ],
        in_specs=[
            whole(length, width), whole(own, width), weight(0), weight(1), weight(2), weight(0),
            whole(length, LANES), whole(length, LANES), whole(own, 1), whole(1, length),
            columns(own), columns(length), columns(length), columns(own), columns(own),
        ],
        out_specs=[
            pl.BlockSpec((1, 3, width, LANES), lambda p: (p // groups, 0, 0, p % groups)),
            weight(0),
            whole(length, width),
        ],
        compiler_params=pltpu.CompilerParams(vmem_limit_bytes=VMEM_LIMIT),
    )(normed, branch, weights, weights, weights, mixing, cosine, sine, seg_rows, seg_cols, *saved)


def rotary_tables(length):
    indices = np.arange(HEAD_SIZE // 2, dtype=np.float32)
    inverse_freq = np.float32(THETA) ** (np.float32(-2.0 / HEAD_SIZE) * indices)
    angles = np.arange(length, dtype=np.float32)[:, None] * inverse_freq[None, :]
    angles = np.tile(angles, (1, LANES // (HEAD_SIZE // 2))).astype(np.float32)
    return jnp.asarray(np.cos(angles)), jnp.asarray(np.sin(angles))


def own_first(rows, core):
    return jnp.where(core == 0, rows, jnp.roll(rows, rows.shape[0] // 2, axis=0))


def per_device(
    doubling,
    inputs,
    segments,
    gain_first,
    gain_second,
    attend_weight,
    mixing_matrix,
    expand_matrix,
    reduce_matrix,
    cotangent,
):
    core = lax.axis_index("tensor")
    own, width = inputs.shape
    length = segments.shape[0]
    share = gain_first.shape[0]
    shards = [attend_weight, mixing_matrix[None], expand_matrix, reduce_matrix[None]]
    cosine, sine = rotary_tables(length)
    segments = own_first(segments, core)
    seg_rows, seg_cols = segments[:own, None], segments[None, :]
    place = (2 * lax.axis_index("dp") + core) * share
    if doubling:
        gains = jnp.zeros((8, width), jnp.float32)
        pair = jnp.stack([gain_first, gain_second])
        gains = lax.dynamic_update_slice(gains, pair, (jnp.int32(0), place))
        output, input_grad, gains, sent_attend, sent_mixing, sent_expand, sent_reduce = layer(
            gains, shards, inputs, cotangent, cosine, sine, seg_rows, seg_cols
        )
        mine = lax.dynamic_slice(gains, (jnp.int32(0), place), (2, share))
        return (
            output, input_grad, mine[0], mine[1], sent_attend, sent_mixing[0], sent_expand,
            sent_reduce[0],
        )
    tables = (own_first(cosine, core), own_first(sine, core), seg_rows, seg_cols)
    both = ("dp", "tensor")
    full_first = lax.all_gather(gain_first, both, axis=0, tiled=True)
    full_second = lax.all_gather(gain_second, both, axis=0, tiled=True)
    attend_full, mixing_full, expand_full, reduce_full = (
        lax.all_gather(lax.all_gather(s, "dp", axis=1, tiled=True), "tensor", axis=0)
        for s in shards
    )
    pair = lax.all_gather(inputs, "tensor", axis=0)
    other_inputs = jnp.where(core == 0, pair[1], pair[0])
    rows_all = jnp.concatenate([inputs, other_inputs]).astype(jnp.float32)
    rows_in = rows_all[:own]
    unit_one, inverse_one = normalize(rows_all)
    normed_one = (unit_one * full_first).astype(jnp.bfloat16)
    saved = attend(normed_one, attend_full, *tables)
    attended = jnp.transpose(saved[3], (1, 0, 2)).reshape(own, width)
    half = attended.shape[1] // 2
    middle = (
        rows_in
        + contract_last(attended[:, :half], mixing_full[0, 0])
        + contract_last(attended[:, half:], mixing_full[1, 0])
    )
    unit_two, inverse_two = normalize(middle)
    normed_two = (unit_two * full_second).astype(jnp.bfloat16)
    output = middle
    grad_normed_two = jnp.zeros_like(middle)
    grad_expand, grad_reduce = [], []
    for side in range(2):
        activated_in = plain(normed_two, expand_full[side, 0])
        gate_linear = plain(normed_two, expand_full[side, 1])
        gelu_value = jax.nn.gelu(activated_in, approximate=False)
        hidden = (gelu_value * gate_linear).astype(jnp.bfloat16)
        output = output + contract_last(hidden, reduce_full[side, 0])
        grad_hidden = plain(cotangent, reduce_full[side, 0])
        grad_reduce.append(contract_first(cotangent, hidden).astype(jnp.bfloat16))
        grad_activated = (grad_hidden * gate_linear * gelu_slope(activated_in)).astype(
            jnp.bfloat16
        )
        grad_gate = (grad_hidden * gelu_value).astype(jnp.bfloat16)
        grad_expand.append(contract_first(normed_two, grad_activated).astype(jnp.bfloat16))
        grad_expand.append(contract_first(normed_two, grad_gate).astype(jnp.bfloat16))
        grad_normed_two = (
            grad_normed_two
            + contract_last(grad_activated, expand_full[side, 0])
            + contract_last(grad_gate, expand_full[side, 1])
        )
    hidden_width = expand_full.shape[3]
    grad_expand = jnp.stack(grad_expand).reshape(2, 2, width, hidden_width)
    grad_reduce = jnp.stack(grad_reduce).reshape(2, 1, width, hidden_width)
    second_local = jnp.sum(grad_normed_two * unit_two, axis=0)
    grad_middle = cotangent.astype(jnp.float32) + normalize_back(
        grad_normed_two * full_second, unit_two, inverse_two
    )
    grad_branch = grad_middle.astype(jnp.bfloat16)
    grad_attend, grad_mixing, grad_normed_one = attend_back(
        normed_one, grad_branch, attend_full, mixing_full, *tables, saved
    )
    first_local = jnp.sum(grad_normed_one * unit_one, axis=0)
    through = normalize_back(grad_normed_one * full_first, unit_one, inverse_one)
    rows_other = through[own:].astype(jnp.bfloat16)

    def summed(part):
        part = part.astype(jnp.float32)
        part = lax.psum_scatter(part, "tensor", scatter_dimension=0, tiled=False)
        return lax.psum_scatter(part, "dp", scatter_dimension=1, tiled=True)

    sent_attend, sent_expand = summed(grad_attend), summed(grad_expand)
    sent_mixing, sent_reduce = summed(grad_mixing)[0], summed(grad_reduce)[0]
    first_grad, second_grad = (
        lax.psum_scatter(part, ("dp", "tensor"), scatter_dimension=0, tiled=True)
        for part in (first_local, second_local)
    )
    pair = lax.all_gather(rows_other, "tensor", axis=0)
    rows_back = jnp.where(core == 0, pair[1], pair[0])
    input_grad = grad_middle + through[:own] + rows_back.astype(jnp.float32)
    return (
        output.astype(jnp.bfloat16),
        input_grad,
        first_grad,
        second_grad,
        sent_attend,
        sent_mixing,
        sent_expand,
        sent_reduce,
    )


def solution(mesh):
    in_specs = (
        P(("dp", "tensor"), None),
        P("dp"),
        P(("dp", "tensor")),
        P(("dp", "tensor")),
        P(None, "dp", "tensor"),
        P("dp", "tensor"),
        P(None, "dp", "tensor"),
        P("dp", "tensor"),
        P(("dp", "tensor"), None),
    )
    out_specs = (
        P(("dp", "tensor"), None),
        P(("dp", "tensor"), None),
        P(("dp", "tensor")),
        P(("dp", "tensor")),
        P(None, "dp", "tensor"),
        P("dp", "tensor"),
        P(None, "dp", "tensor"),
        P("dp", "tensor"),
    )
    doubling = mesh.shape["dp"] == 16 and mesh.shape["tensor"] == 2
    return jax.shard_map(
        functools.partial(per_device, doubling),
        mesh=mesh,
        in_specs=in_specs,
        out_specs=out_specs,
        check_vma=False,
    )
```

profile of v0, /device:TPU:0, one launch (start us, length us, event | category | flops | bytes accessed | tf_op | source)
XLA Modules:
  0.0 165.3 jit_solution(7070290739297991855)
XLA Ops:
  0.6 0.0 copy-start.8
  0.7 0.0 copy-start.9
  0.7 0.0 copy-start.7
  0.7 0.6 copy-done.8
  1.3 0.0 copy-done.9
  1.3 0.0 copy-done.7
  1.4 0.0 copy-start.6
  1.4 0.6 copy-done.6
  2.0 0.2 dynamic_update_slice.3.gain_part
  2.2 0.0 copy-start.4
  2.2 0.8 copy.19.seg_rows
  3.0 0.0 copy-done.4
  3.0 154.8 %shard_map.170 = (bf16[256,768]{1,0:T(8,128)(2,1)}, f32[256,768]{1,0:T(8,128)}, f32[8,768]{1,0:T(8,128)}, f32[3,48,384]{2,1,0:T(8,128)}, f32[1,48,384]{2,1,0:T(8...) custom-call(f32[8,768]{1,0:T(8,128)} %copy-done.4, bf16[3,48,384]{2,1,0:T(8,128)(2,1)} %attend_w.1, ...), custom_call_target="tpu_custom_call" | custom-call | tf_op jit(solution)/shard_map/pallas_call | solution.py:510
  157.8 0.0 copy-start
  157.8 0.8 constant_dynamic-slice_fusion
  158.7 0.5 slice_bitcast_fusion
  159.2 1.8 %copy.27 = bf16[256,768]{1,0:T(8,128)(2,1)} copy(bf16[256,768]{1,0:T(8,128)(2,1)} %get-tuple-element.34) | data formatting | bytes 786432
  161.0 0.0 copy-done
  161.0 0.0 copy-start.2
  161.0 0.9 copy.28
  161.9 0.3 copy-done.2
  162.1 0.0 copy-start.5
  162.1 0.0 copy-start.1
  162.1 0.7 copy.29
  162.8 0.2 copy-done.5
  163.0 0.6 copy.30
  163.7 0.0 copy-done.1
  163.7 0.0 copy-start.3
  163.7 0.7 copy.31
  164.4 0.3 copy-done.3
  164.7 0.6 copy.32
  (5 shorter events, 0.0 us)
Async XLA Ops:
  0.6 0.7 copy-start.8
  0.7 0.7 copy-start.9
  0.7 0.7 copy-start.7
  1.4 0.6 copy-start.6
  2.2 0.8 copy-start.4
  157.8 3.1 %copy-start = (f32[256,768]{1,0:T(8,128)S(1)}, f32[256,768]{1,0:T(8,128)}, u32[]{:S(2)}) copy-start(f32[256,768]{1,0:T(8,128)} %get-tuple-element.35) | copy-start | bytes 2359300
  161.0 1.1 copy-start.2
  162.1 0.9 copy-start.5
  162.1 1.5 copy-start.1
  163.7 1.0 copy-start.3
where the time goes:
time: 166 us; the launch traced here: 165 us
  Pallas kernels  155 us (93%)
  local copies, waits for them, and re-layouts  9.76 us (6%)
    pallas_call x1, Pallas kernels, layer(): pl.pallas_call(layer_kernel, out_shape=[jax.ShapeDtypeStruct((own, width)...  155 us
    unnamed x26, local copies, waits for them, and re-layouts  7.34 us

commit v1 on v0

--- a/solution.py
+++ b/solution.py
@@ -129,9 +129,6 @@
         totals[i] = (start[...] if i == 0 else totals[i - 1]) + arrived[i]
 
     return Chunk(groups, landed)
-
-
-LAG = 2
 
 
 def gather_groups(remote, k, shard, full, j, route, at):
@@ -334,10 +331,12 @@
             summed = summed + contract_last(jnp.concatenate(columns, axis=1), weight)
         middle[...] = summed
 
-    events = [(k + LAG * s, chunk.advance) for k, chunk in enumerate(chunks) for s in range(6)]
-    events += [(4.5, own_unit), (7.5, other_unit), (5 * LAG + 0.5, norm)]
-    begin = 3 + 5 * LAG
-    events += [(begin + 0.1 + 0.65 * p, heads(p)) for p in range(pairs)] + [(begin + 3.6, mix)]
+    offsets = (0, 1, 2, 3) + tuple(11.5 + 2 * i for i in range(4))
+    events = [
+        (offset + 4 * s, chunk.advance) for offset, chunk in zip(offsets, chunks) for s in range(6)
+    ]
+    events += [(5.5, own_unit), (9.5, other_unit), (20.5, norm)]
+    events += [(23.1 + 1.6 * p, heads(p)) for p in range(pairs)] + [(23.2 + 1.6 * pairs, mix)]
     for _, event in sorted(events, key=lambda e: e[0]):
         event()
 
@@ -563,7 +562,7 @@
         peak = jnp.max(scores, axis=-1, keepdims=True)
         exponent = jnp.exp(scores - peak)
         total = jnp.sum(exponent, axis=-1, keepdims=True)
-        probs = (exponent / total).astype(jnp.bfloat16)
+        probs = (exponent * (1.0 / total)).astype(jnp.bfloat16)
         mixed.append(plain(probs, value[:, part]).astype(jnp.bfloat16))
         logs.append(jnp.broadcast_to(peak + jnp.log(total), (own, HEAD_SIZE)))
     return query, keys, value, jnp.concatenate(mixed, axis=1), jnp.concatenate(logs, axis=1)

time: 166 us -> 162 us (0.976)
  Pallas kernels: 155 us -> 151 us
    pallas_call x1, Pallas kernels: 155 us -> 151 us  [layer(): pl.pallas_call(layer_kernel, out_shape=[jax.ShapeDtypeStruct((own, width)...]
where the time goes in v1:
time: 162 us; the launch traced here: 161 us
  Pallas kernels  151 us (93%)
  local copies, waits for them, and re-layouts  9.76 us (6%)
    pallas_call x1, Pallas kernels, layer(): pl.pallas_call(layer_kernel, out_shape=[jax.ShapeDtypeStruct((own, width)...  151 us
    unnamed x26, local copies, waits for them, and re-layouts  7.34 us

profile of v1, /device:TPU:0, one launch (start us, length us, event | category | flops | bytes accessed | tf_op | source)
XLA Modules:
  0.0 161.5 jit_solution(11074113215414080649)
XLA Ops:
  0.6 0.0 copy-start.8
  0.7 0.0 copy-start.9
  0.7 0.0 copy-start.7
  0.7 0.6 copy-done.8
  1.3 0.0 copy-done.9
  1.3 0.0 copy-done.7
  1.4 0.0 copy-start.6
  1.4 0.6 copy-done.6
  2.0 0.2 dynamic_update_slice.3.gain_part
  2.2 0.0 copy-start.4
  2.2 0.8 copy.19.seg_rows
  3.0 0.0 copy-done.4
  3.0 151.0 %shard_map.170 = (bf16[256,768]{1,0:T(8,128)(2,1)}, f32[256,768]{1,0:T(8,128)}, f32[8,768]{1,0:T(8,128)}, f32[3,48,384]{2,1,0:T(8,128)}, f32[1,48,384]{2,1,0:T(8...) custom-call(f32[8,768]{1,0:T(8,128)} %copy-done.4, bf16[3,48,384]{2,1,0:T(8,128)(2,1)} %attend_w.1, ...), custom_call_target="tpu_custom_call" | custom-call | tf_op jit(solution)/shard_map/pallas_call | solution.py:509
  154.0 0.0 copy-start
  154.0 0.8 constant_dynamic-slice_fusion
  154.9 0.5 slice_bitcast_fusion
  155.4 1.8 %copy.27 = bf16[256,768]{1,0:T(8,128)(2,1)} copy(bf16[256,768]{1,0:T(8,128)(2,1)} %get-tuple-element.34) | data formatting | bytes 786432
  157.2 0.0 copy-done
  157.2 0.0 copy-start.2
  157.2 0.9 copy.28
  158.0 0.3 copy-done.2
  158.3 0.0 copy-start.5
  158.3 0.0 copy-start.1
  158.3 0.7 copy.29
  159.0 0.2 copy-done.5
  159.2 0.6 copy.30
  159.8 0.0 copy-done.1
  159.8 0.0 copy-start.3
  159.9 0.7 copy.31
  160.5 0.3 copy-done.3
  160.8 0.6 copy.32
  (5 shorter events, 0.0 us)
Async XLA Ops:
  0.6 0.7 copy-start.8
  0.7 0.7 copy-start.9
  0.7 0.7 copy-start.7
  1.4 0.6 copy-start.6
  2.2 0.8 copy-start.4
  154.0 3.1 %copy-start = (f32[256,768]{1,0:T(8,128)S(1)}, f32[256,768]{1,0:T(8,128)}, u32[]{:S(2)}) copy-start(f32[256,768]{1,0:T(8,128)} %get-tuple-element.35) | copy-start | bytes 2359300
  157.2 1.1 copy-start.2
  158.3 0.9 copy-start.5
  158.3 1.5 copy-start.1
  159.8 1.0 copy-start.3
